TPU v7x, 32 devices: a whole 2x2x4 slice. The times are simulated.
32 devices in a mesh: rows: 4 (over x, core), vec: 8 (over z, y).
Axes of the slice: x: 2, y: 2, z: 4, core: 2. Of those that a mesh axis runs over, the one named last changes fastest.
Arguments:
- eigen_rows: float32 [2048, 1024], P('rows', 'vec'), may hold values from -6 to 6
- panels: float32 [3, 2048, 256], P(None, ('rows', 'vec')), may hold values from -0.25 to 0.25
Outputs:
- transformed: float32 [2048, 1024], P('rows', 'vec')
All inputs are finite; a program needn't handle non-finite values.
Results may differ from a plain program's by a relative error of at most 0.00017.
Values sent between devices are 32-bit elements; how exact they have to be, the bound alone decides.
A program may use at most 192 MiB of HBM per device.

v0:
```python
import jax
import jax.numpy as jnp
from jax import lax
from jax.sharding import PartitionSpec as P

REFLECTORS = 256
SLOTS = 3


def shifted_2(block, axis, distance):
    devices = range(lax.axis_size(axis))
    route = [(i - distance, i) for i in devices if i - distance in devices]
    return lax.ppermute(block, axis, route)


def invert_upper(triangle):
    width = triangle.shape[-1]
    lead = triangle.shape[:-2]
    diag_vals = jnp.diagonal(triangle, axis1=-2, axis2=-1)
    inverse_blocks = (1.0 / diag_vals).reshape(lead + (width, 1, 1))
    span = 1
    while span < width:
        count = width // (2 * span)
        tiles = triangle.reshape(lead + (count, 2 * span, count, 2 * span))
        own_tiles = jnp.einsum("...mimj->...mij", tiles)
        corner = own_tiles[..., :span, span:]
        upper_inv = inverse_blocks[..., 0::2, :, :]
        lower_inv = inverse_blocks[..., 1::2, :, :]
        middle = jnp.einsum(
            "...mij,...mjk->...mik", upper_inv, corner, precision=lax.Precision.HIGHEST
        )
        middle = -jnp.einsum(
            "...mij,...mjk->...mik", middle, lower_inv, precision=lax.Precision.HIGHEST
        )
        top_half = jnp.concatenate([upper_inv, middle], axis=-1)
        bottom_half = jnp.concatenate([jnp.zeros_like(lower_inv), lower_inv], axis=-1)
        inverse_blocks = jnp.concatenate([top_half, bottom_half], axis=-2)
        span = span * 2
    return inverse_blocks.reshape(lead + (width, width))


def reflect(panel_rows, values):
    block_len = panel_rows.shape[-2]
    width = panel_rows.shape[-1]
    shifted = panel_rows + jnp.eye(block_len, width, dtype=panel_rows.dtype)
    inner_products = jnp.einsum(
        "...br,...bs->...rs", shifted, shifted, precision=lax.Precision.HIGHEST
    )
    triangle = jnp.triu(inner_products, 1) + 0.5 * inner_products * jnp.eye(
        width, dtype=panel_rows.dtype
    )
    projected = jnp.einsum("...br,...bc->...rc", shifted, values, precision=lax.Precision.HIGHEST)
    inverse = invert_upper(triangle)
    solved = jnp.einsum("...rs,...sc->...rc", inverse, projected, precision=lax.Precision.HIGHEST)
    return values - jnp.einsum(
        "...br,...rc->...bc", shifted, solved, precision=lax.Precision.HIGHEST
    )


def apply_blocks(panel_rows, values):
    block_len = 2 * REFLECTORS
    pieces = values.shape[0] // block_len
    columns = values.shape[1]
    applied = reflect(
        panel_rows.reshape(pieces, block_len, REFLECTORS),
        values.reshape(pieces, block_len, columns),
    )
    return applied.reshape(pieces * block_len, columns)


def local(eigen_rows, panels):
    group_rows = eigen_rows.shape[0]
    columns = eigen_rows.shape[1]
    group_index = lax.axis_index("rows")
    group_count = lax.axis_size("rows")
    values = eigen_rows
    for sweep_set in range(SLOTS):
        current = lax.all_gather(panels[sweep_set], "vec", axis=0, tiled=True)
        if sweep_set % 2 == 0:
            values = apply_blocks(current, values)
        else:
            top_rims = jnp.concatenate([values[:REFLECTORS], current[:REFLECTORS]], axis=1)
            lower_rims = shifted_2(top_rims, "rows", -1)
            local_values = jnp.concatenate([values[REFLECTORS:], lower_rims[:, :columns]], axis=0)
            local_panels = jnp.concatenate([current[REFLECTORS:], lower_rims[:, columns:]], axis=0)
            applied = apply_blocks(local_panels, local_values)
            own_rows = applied[: group_rows - REFLECTORS]
            row_numbers = lax.broadcasted_iota(jnp.int32, (group_rows - REFLECTORS, 1), 0)
            keep_last = jnp.logical_and(
                row_numbers >= group_rows - 2 * REFLECTORS, group_index == group_count - 1
            )
            own_rows = jnp.where(keep_last, values[REFLECTORS:], own_rows)
            returned = shifted_2(applied[group_rows - REFLECTORS :], "rows", 1)
            first_rows = jnp.where(group_index == 0, values[:REFLECTORS], returned)
            values = jnp.concatenate([first_rows, own_rows], axis=0)
    return values


def solution(mesh):
    in_specs = (P("rows", "vec"), P(None, ("rows", "vec"), None))
    out_specs = P("rows", "vec")
    return jax.shard_map(local, mesh=mesh, in_specs=in_specs, out_specs=out_specs, check_vma=False)
```

profile of v0, /device:TPU:1, one launch (start us, length us, event | category | flops | bytes accessed | tf_op | source)
XLA Modules:
  0.0 299.8 jit_solution(3726397549032323212)
XLA Ops:
  0.0 1.5 fusion.181
  1.5 26.9 %all-gather = f32[1,512,256]{2,1,0:T(8,128)S(1)} all-gather(f32[1,64,256]{2,1,0:T(8,128)S(1)} %get-tuple-element.25), channel_id=2, replica_groups=mesh['rows'=4,'vec'=8] {'vec'}, dimensions={1}, use_global_device_ids=true | all-gather | bytes 589824 | tf_op jit(solution)/shard_map/all_gather | solution.py:78
  28.5 1.0 select_add_fusion.2
  29.5 2.3 gather_fusion
  32.1 0.7 slice.270
  32.8 18.1 %reshape.864 = f32[1,128,2,128,2]{4,3,2,1,0:T(8,128)} reshape(f32[256,256]{1,0:T(8,128)S(1)} %select_add_fusion.2) | data formatting | bytes 524288 | tf_op jit(solution)/shard_map/reshape | solution.py:24
  50.9 0.6 iota_compare_fusion.14
  51.5 10.0 %reshape.866 = f32[1,64,4,64,4]{4,3,2,1,0:T(8,128)} reshape(f32[256,256]{1,0:T(8,128)S(1)} %select_add_fusion.2) | data formatting | bytes 524288 | tf_op jit(solution)/shard_map/reshape | solution.py:24
  61.5 3.6 %reshape.870 = f32[1,32,8,32,8]{4,3,2,1,0:T(8,128)} reshape(f32[256,256]{1,0:T(8,128)S(1)} %select_add_fusion.2) | data formatting | bytes 524288 | tf_op jit(solution)/shard_map/reshape | solution.py:24
  65.2 0.6 reshape.874
  65.8 0.6 iota_compare_fusion.17
  66.4 1.3 reshape.878
  67.7 0.6 iota_compare_fusion.18
  69.0 0.9 reshape.886
  69.9 0.6 iota_compare_fusion.20
  70.5 25.5 %all-gather.1 = f32[1,512,256]{2,1,0:T(8,128)S(1)} all-gather(f32[1,64,256]{2,1,0:T(8,128)S(1)} %get-tuple-element.27), channel_id=3, replica_groups=mesh['rows'=4,'vec'=8] {'vec'}, dimensions={1}, use_global_device_ids=true | all-gather | bytes 589824 | tf_op jit(solution)/shard_map/all_gather | solution.py:78
  96.0 0.8 slice_bitcast_fusion
  96.8 2.6 fusion.23
  99.5 0.7 copy.231
  100.2 7.0 %select_reduce_fusion.2 = f32[2,128,2]{2,1,0:T(8,128)S(1)} fusion(f32[1,128,2,128,2]{4,3,2,1,0:T(8,128)} %reshape.864, pred[128,128]{1,0:T(8,128)(4,1)} %iota_compare_fusion.14), kind=kLoop, calls=%fused_computation.5 | loop fusion | flops 130560 | bytes 280576 | tf_op jit(solution)/shard_map/...mimj->...mij/reduce_sum | solution.py:25
  107.9 4.3 %select_reduce_fusion.5 = f32[4,64,4]{2,1,0:T(8,128)S(1)} fusion(f32[1,64,4,64,4]{4,3,2,1,0:T(8,128)} %reshape.866, pred[64,64]{1,0:T(8,128)(4,1)S(1)} %iota_compare_fusion.15), kind=kLoop, calls=%fused_computation.8 | loop fusion | flops 130048 | bytes 270336 | tf_op jit(solution)/shard_map/...mimj->...mij/reduce_sum | solution.py:25
  112.3 0.6 fusion.121
  119.8 0.6 fusion.1
  120.4 0.8 pad_maximum_fusion
  121.2 14.0 %collective-permute-start = (f32[256,384]{1,0:T(8,128)}, f32[256,384]{1,0:T(8,128)}, u32[]{:S(2)}, u32[]{:S(2)}) collective-permute-start(f32[256,384]{1,0:T(8,128)} %pad_maximum_fusion), channel_id=1, source_target_pairs={{8,0},{16,8},{24,16},{9,1},{17,9},{25,17},{10,2},{18,10},{26,18},{... | collective-permute-start | bytes 1179656 | tf_op jit(solution)/shard_map/ppermute | solution.py:13
  135.3 26.0 %all-gather.2 = f32[1,512,256]{2,1,0:T(8,128)S(1)} all-gather(f32[1,64,256]{2,1,0:T(8,128)S(1)} %copy-done.21), channel_id=4, replica_groups=mesh['rows'=4,'vec'=8] {'vec'}, dimensions={1}, use_global_device_ids=true | all-gather | bytes 589824 | tf_op jit(solution)/shard_map/all_gather | solution.py:78
  161.2 1.0 select_add_fusion
  162.3 18.3 %reshape.922 = f32[1,128,2,128,2]{4,3,2,1,0:T(8,128)} reshape(f32[256,256]{1,0:T(8,128)S(1)} %select_add_fusion) | data formatting | bytes 524288 | tf_op jit(solution)/shard_map/reshape | solution.py:24
  180.6 10.0 %reshape.924 = f32[1,64,4,64,4]{4,3,2,1,0:T(8,128)} reshape(f32[256,256]{1,0:T(8,128)S(1)} %select_add_fusion) | data formatting | bytes 524288 | tf_op jit(solution)/shard_map/reshape | solution.py:24
  190.6 3.7 %reshape.928 = f32[1,32,8,32,8]{4,3,2,1,0:T(8,128)} reshape(f32[256,256]{1,0:T(8,128)S(1)} %select_add_fusion) | data formatting | bytes 524288 | tf_op jit(solution)/shard_map/reshape | solution.py:24
  194.2 0.6 reshape.932
  194.9 1.3 reshape.936
  196.1 1.0 reshape.940
  197.2 0.8 reshape.944
  198.0 2.3 gather_fusion.2
  200.8 0.7 copy.236
  201.6 0.7 copy.235
  202.3 1.0 slice.379
  203.3 2.1 select_add_fusion.1
  205.3 2.9 gather_fusion.1
  208.3 0.7 broadcast_divide_fusion.1
  209.0 0.8 slice.305
  209.7 0.8 slice.303
  210.5 18.1 %reshape.893 = f32[1,128,2,128,2]{4,3,2,1,0:T(8,128)} reshape(f32[256,256]{1,0:T(8,128)S(1)} %select_add_fusion.1) | data formatting | bytes 524288 | tf_op jit(solution)/shard_map/reshape | solution.py:24
  228.6 9.9 %reshape.895 = f32[1,64,4,64,4]{4,3,2,1,0:T(8,128)} reshape(f32[256,256]{1,0:T(8,128)S(1)} %select_add_fusion.1) | data formatting | bytes 524288 | tf_op jit(solution)/shard_map/reshape | solution.py:24
  238.5 3.6 %reshape.899 = f32[1,32,8,32,8]{4,3,2,1,0:T(8,128)} reshape(f32[256,256]{1,0:T(8,128)S(1)} %select_add_fusion.1) | data formatting | bytes 524288 | tf_op jit(solution)/shard_map/reshape | solution.py:24
  242.1 2.0 reshape.903
  244.1 1.2 reshape.907
  245.4 1.0 reshape.911
  246.4 0.8 reshape.915
  247.2 1.4 copy.234
  248.6 0.7 copy.233
  249.3 13.4 %select_reduce_fusion = (f32[2,128,2]{2,1,0:T(8,128)S(1)}, f32[2,128,2]{2,1,0:T(8,128)S(1)}) fusion(f32[1,128,2,128,2]{4,3,2,1,0:T(8,128)} %reshape.922, pred[128,128]{1,0:T(8,128)(4,1)} %iota_compare_fusion.14, f32[1,128,2,128,2]{4,3,2,1,0:T(8,128)} %reshape.893), kind=kLoop, calls=%fused_computation.3 | loop fusion | flops 261120 | bytes 544768 | tf_op jit(solution)/shard_map/...mimj->...mij/reduce_sum | solution.py:25
  263.6 7.2 %select_reduce_fusion.3 = (f32[4,64,4]{2,1,0:T(8,128)S(1)}, f32[4,64,4]{2,1,0:T(8,128)S(1)}) fusion(f32[1,64,4,64,4]{4,3,2,1,0:T(8,128)} %reshape.924, pred[64,64]{1,0:T(8,128)(4,1)S(1)} %iota_compare_fusion.15, f32[1,64,4,64,4]{4,3,2,1,0:T(8,128)} %reshape.895), kind=kLoop, calls=%fused_computation.6 | loop fusion | flops 260096 | bytes 536576 | tf_op jit(solution)/shard_map/...mimj->...mij/reduce_sum | solution.py:25
  271.0 0.6 fusion.106
  272.5 1.0 select_reduce_fusion.6
  279.6 0.9 slice.377
  280.5 1.0 fusion.48
  281.9 0.6 fusion
  282.5 8.5 %collective-permute-start.1 = (f32[256,128]{1,0:T(8,128)S(1)}, f32[256,128]{1,0:T(8,128)S(1)}, u32[]{:S(2)}, u32[]{:S(2)}) collective-permute-start(f32[256,128]{1,0:T(8,128)S(1)} %slice_bitcast_fusion.3), channel_id=1, source_target_pairs={{0,8},{8,16},{16,24},{1,9},{9,17},{17,25},{2,10},{10,18},{18,26},{... | collective-permute-start | bytes 393224 | tf_op jit(solution)/shard_map/ppermute | solution.py:13
  291.6 0.6 fusion.91
  292.3 0.6 fusion.8
  297.0 1.0 fusion.25
  298.3 1.3 convolution_subtract_fusion
  (189 shorter events, 21.6 us)
Async XLA Ops:
  107.9 5.8 %copy-start = (f32[1,32,8,32,8]{4,3,2,1,0:T(8,128)S(1)}, f32[1,32,8,32,8]{4,3,2,1,0:T(8,128)}, u32[]{:S(2)}) copy-start(f32[1,32,8,32,8]{4,3,2,1,0:T(8,128)} %reshape.870) | copy-start | bytes 786436
  112.2 3.2 %copy-start.23 = (pred[16,16]{1,0:T(8,128)(4,1)S(1)}, pred[16,16]{1,0:T(8,128)(4,1)}, u32[]{:S(2)}) copy-start(pred[16,16]{1,0:T(8,128)(4,1)} %iota_compare_fusion.17) | copy-start | bytes 772
  113.7 2.7 copy-start.6
  113.7 2.7 copy-start.25
  114.3 3.0 copy-start.29
  115.2 2.9 copy-start.14
  115.2 2.9 copy-start.27
  115.7 3.7 %copy-start.22 = (f32[256,128]{1,0:T(8,128)S(1)}, f32[256,128]{1,0:T(8,128)}, u32[]{:S(2)}) copy-start(f32[256,128]{1,0:T(8,128)} %fusion.23) | copy-start | bytes 393220
  115.7 4.1 %copy-start.12 = (f32[512,128]{1,0:T(8,128)S(1)}, f32[512,128]{1,0:T(8,128)}, u32[]{:S(2)}) copy-start(f32[512,128]{1,0:T(8,128)} %param.2) | copy-start | bytes 786436
  116.5 4.0 %copy-start.13 = (f32[256,256]{1,0:T(8,128)S(1)}, f32[256,256]{1,0:T(8,128)}, u32[]{:S(2)}) copy-start(f32[256,256]{1,0:T(8,128)} %get-tuple-element.20) | copy-start | bytes 786436
  116.6 18.6 %copy-start.21 = (f32[1,64,256]{2,1,0:T(8,128)S(1)}, f32[1,64,256]{2,1,0:T(8,128)}, u32[]{:S(2)}) copy-start(f32[1,64,256]{2,1,0:T(8,128)} %get-tuple-element.26) | copy-start | bytes 196612
  120.4 14.9 %copy-start.8 = (f32[1,512,128]{2,1,0:T(8,128)}, f32[1,512,128]{2,1,0:T(8,128)S(1)}, u32[]{:S(2)}) copy-start(f32[1,512,128]{2,1,0:T(8,128)S(1)} %fusion.1) | copy-start | bytes 786436
  121.2 81.1 %collective-permute-start = (f32[256,384]{1,0:T(8,128)}, f32[256,384]{1,0:T(8,128)}, u32[]{:S(2)}, u32[]{:S(2)}) collective-permute-start(f32[256,384]{1,0:T(8,128)} %pad_maximum_fusion), channel_id=1, source_target_pairs={{8,0},{16,8},{24,16},{9,1},{17,9},{25,17},{10,2},{18,10},{26,18},{... | collective-permute-start | bytes 1179656 | tf_op jit(solution)/shard_map/ppermute | solution.py:13
  238.5 10.1 %copy-start.31 = (f32[1,128,1,1]{1,3,2,0:T(1,128)S(1)}, f32[1,128,1,1]{1,3,2,0:T(1,128)}, u32[]{:S(2)}) copy-start(f32[1,128,1,1]{1,3,2,0:T(1,128)} %slice.303) | copy-start | bytes 1540
  249.3 13.6 %copy-start.19 = (f32[1,128,1,1]{3,2,1,0:T(1,128)S(1)}, f32[1,128,1,1]{3,2,1,0:T(1,128)}, u32[]{:S(2)}) copy-start(f32[1,128,1,1]{3,2,1,0:T(1,128)} %copy.234) | copy-start | bytes 1540
  249.3 13.6 %copy-start.20 = (f32[1,128,1,1]{3,2,1,0:T(1,128)S(1)}, f32[1,128,1,1]{3,2,1,0:T(1,128)}, u32[]{:S(2)}) copy-start(f32[1,128,1,1]{3,2,1,0:T(1,128)} %copy.233) | copy-start | bytes 1540
  263.6 8.9 %copy-start.1 = (f32[1,32,8,32,8]{4,3,2,1,0:T(8,128)S(1)}, f32[1,32,8,32,8]{4,3,2,1,0:T(8,128)}, u32[]{:S(2)}) copy-start(f32[1,32,8,32,8]{4,3,2,1,0:T(8,128)} %reshape.928) | copy-start | bytes 786436
  263.6 8.9 %copy-start.2 = (f32[1,32,8,32,8]{4,3,2,1,0:T(8,128)S(1)}, f32[1,32,8,32,8]{4,3,2,1,0:T(8,128)}, u32[]{:S(2)}) copy-start(f32[1,32,8,32,8]{4,3,2,1,0:T(8,128)} %reshape.899) | copy-start | bytes 786436
  272.4 2.2 copy-start.3
  272.4 2.2 copy-start.24
  273.5 2.6 copy-start.4
  273.5 2.6 copy-start.5
  273.5 2.6 copy-start.26
  274.6 2.4 copy-start.10
  274.6 2.4 copy-start.11
  274.7 2.4 copy-start.30
  275.2 2.9 copy-start.15
  275.2 2.9 copy-start.16
  275.2 2.9 copy-start.28
  276.4 4.1 %copy-start.7 = (f32[256,256]{1,0:T(8,128)S(1)}, f32[256,256]{1,0:T(8,128)}, u32[]{:S(2)}) copy-start(f32[256,256]{1,0:T(8,128)} %get-tuple-element.19) | copy-start | bytes 786436
  277.0 14.0 %copy-start.17 = (f32[1,128,1,1]{3,2,1,0:T(1,128)S(1)}, f32[1,128,1,1]{3,2,1,0:T(1,128)}, u32[]{:S(2)}) copy-start(f32[1,128,1,1]{3,2,1,0:T(1,128)} %copy.236) | copy-start | bytes 1540
  277.1 14.0 %copy-start.18 = (f32[1,128,1,1]{3,2,1,0:T(1,128)S(1)}, f32[1,128,1,1]{3,2,1,0:T(1,128)}, u32[]{:S(2)}) copy-start(f32[1,128,1,1]{3,2,1,0:T(1,128)} %copy.235) | copy-start | bytes 1540
  281.9 15.0 %copy-start.9 = (f32[1,512,128]{2,1,0:T(8,128)S(1)}, f32[1,512,128]{2,1,0:T(8,128)}, u32[]{:S(2)}) copy-start(f32[1,512,128]{2,1,0:T(8,128)} %copy-done.8) | copy-start | bytes 786436
  282.5 14.4 %collective-permute-start.1 = (f32[256,128]{1,0:T(8,128)S(1)}, f32[256,128]{1,0:T(8,128)S(1)}, u32[]{:S(2)}, u32[]{:S(2)}) collective-permute-start(f32[256,128]{1,0:T(8,128)S(1)} %slice_bitcast_fusion.3), channel_id=1, source_target_pairs={{0,8},{8,16},{16,24},{1,9},{9,17},{17,25},{2,10},{10,18},{18,26},{... | collective-permute-start | bytes 393224 | tf_op jit(solution)/shard_map/ppermute | solution.py:13
where the time goes:
time: 305 us; the launch traced here: 300 us
  local copies, waits for them, and re-layouts  128 us (42%)
  blocking collectives  78.3 us (26%)
  other arithmetic  44.2 us (14%)
  matrix products  25.2 us (8%)
  starting transfers between devices  22.5 us (7%)
    reshape x21, local copies, waits for them, and re-layouts, invert_upper(): tiles = triangle.reshape(lead + (count, 2 * span, count, 2 * span))  107 us
    all_gather x3, blocking collectives, local(): current = lax.all_gather(panels[sweep_set], 'vec', axis=0, tiled=True)  78.3 us
    reduce_sum x14, other arithmetic, invert_upper(): own_tiles = jnp.einsum('...mimj->...mij', tiles)  35.9 us
    ppermute x2, starting transfers between devices, shifted_2(): return lax.ppermute(block, axis, route)  22.5 us
    gather x3, local copies, waits for them, and re-layouts, invert_upper(): diag_vals = jnp.diagonal(triangle, axis1=-2, axis2=-1)  7.63 us
    dot_general x21, matrix products, invert_upper(): jnp.einsum('...mij,...mjk->...mik', upper_inv, corner, precision=lax.Prec...  7.02 us
  transfers between devices with their start and end apart: 2, of which 0 were waited for; matrix products, arithmetic and copies ran while one was open for 16% of the time, Pallas kernels for 0%

commit v1 on v0

v1 whole, which is shorter than its diff:
```python
import functools

import jax
import jax.numpy as jnp
from jax import lax
from jax.experimental import pallas as pl
from jax.experimental.pallas import tpu as pltpu
from jax.sharding import PartitionSpec as P

MESH = pl.DeviceIdType.MESH
BASE = 8
F32, BF16 = jnp.float32, jnp.bfloat16


def split(a):
    high = a.astype(BF16)
    return high, (a - high.astype(F32)).astype(BF16)


def mm(a, b):
    ah, al = a
    bh, bl = b
    n = bh.shape[1]
    if n % 256:
        both = jnp.concatenate([bh, bl], axis=1)
        left = jnp.concatenate([ah, al], axis=1)
        out = jnp.dot(
            left, jnp.concatenate([both, both], axis=0), preferred_element_type=F32
        )
        return out[:, :n] + out[:, n:]
    dot = functools.partial(jnp.dot, preferred_element_type=F32)
    return dot(ah, bh) + (dot(ah, bl) + dot(al, bh))


def eye_of(rows, cols):
    r = lax.broadcasted_iota(jnp.int32, (rows, cols), 0)
    c = lax.broadcasted_iota(jnp.int32, (rows, cols), 1)
    return jnp.where(r == c, 1.0, 0.0).astype(F32)


def invert_all(grams):
    width = grams[0].shape[0]
    half = width // 2
    r = lax.broadcasted_iota(jnp.int32, (half, half), 0)
    c = lax.broadcasted_iota(jnp.int32, (half, half), 1)
    eye = jnp.where(r == c, 1.0, 0.0).astype(F32)
    parts, corners, scales = [], [], []
    for g in grams:
        d_rows = []
        d_cols = []
        for i in range(2):
            tile = g[i * half : (i + 1) * half, i * half : (i + 1) * half]
            diag = jnp.where(r == c, 0.5 * tile, 0.0)
            d_rows.append(1.0 / jnp.sum(diag, axis=0, keepdims=True))
            d_cols.append(1.0 / jnp.sum(diag, axis=1, keepdims=True))
            parts.append(jnp.where(c > r, tile * d_rows[i], 0.0))
        corners.append(g[:half, half:] * d_rows[1])
        scales.append(d_cols)
    small = [jnp.where(r // BASE == c // BASE, m, 0.0) for m in parts]
    pairs = [split(m) for m in small]
    powers = [mm(p, p) for p in pairs]
    inv = [eye - m for m in small]
    span = 2
    while span < BASE:
        pairs = [split(p) for p in powers]
        inv = [i + mm(split(i), p) for i, p in zip(inv, pairs)]
        span *= 2
        if span < BASE:
            powers = [mm(p, p) for p in pairs]
        else:
            break
    span = BASE
    while span < half:
        mask = jnp.logical_and(r // (2 * span) == c // (2 * span), r // span != c // span)
        cross = [split(jnp.where(mask, m, 0.0)) for m in parts]
        pairs = [split(i) for i in inv]
        mid = [mm(x, p) for x, p in zip(cross, pairs)]
        inv = [i - mm(p, split(m)) for i, p, m in zip(inv, pairs, mid)]
        span *= 2
    pairs = [split(i) for i in inv]
    mids = [mm(split(corners[k]), pairs[2 * k + 1]) for k in range(len(grams))]
    tops = [-mm(pairs[2 * k], split(mids[k])) for k in range(len(grams))]
    out = []
    for k in range(len(grams)):
        upper = jnp.concatenate([inv[2 * k], tops[k]], axis=1) * scales[k][0]
        lower = jnp.concatenate([jnp.zeros_like(tops[k]), inv[2 * k + 1]], axis=1) * scales[k][1]
        out.append(jnp.concatenate([upper, lower], axis=0))
    return out


def kernel(n, ng, z_ref, p_ref, out_ref, ybuf, gsend, grecv, wsend, wrecv,
           local_sem, send_sem, recv_sem, gs_sem, gr_sem, ws_sem, wr_sem):
    sets, shard, width = p_ref.shape
    steps = n // 2
    hw = width // 2
    g = lax.axis_index("rows")
    me = lax.axis_index("vec")
    odd = me % 2
    pos = (1 - odd) * (me // 2) + odd * (n - 1 - me // 2)

    def index_of(q):
        q = (q + 2 * n) % n
        first = 1 - (2 * q) // n
        return first * (2 * q) + (1 - first) * (2 * (n - 1 - q) + 1)

    sides = (index_of(pos + 1), index_of(pos - 1))
    has_up = g < ng - 1
    has_down = g > 0

    def slot(s, q, t, way):
        rows = pl.ds(pl.multiple_of(index_of(q) * shard, shard), shard)
        if t < steps - 1:
            return ybuf.at[s, rows, :]
        return ybuf.at[s, rows, pl.ds(way * hw, hw)]

    def sent(s, t, way):
        sign = 1 - 2 * way
        ref = slot(s, pos - sign * t, t, way)
        src = p_ref.at[s] if t == 0 and steps > 1 else ref
        return pltpu.make_async_remote_copy(
            src_ref=src, dst_ref=ref,
            send_sem=send_sem.at[s, way, t], recv_sem=recv_sem.at[s, way, t],
            device_id={"vec": sides[way]}, device_id_type=MESH)

    def arrived(s, t, way):
        sign = 1 - 2 * way
        ref = slot(s, pos - sign * (t + 1), t, way)
        return pltpu.make_async_remote_copy(
            src_ref=ref, dst_ref=ref,
            send_sem=send_sem.at[s, way, t], recv_sem=recv_sem.at[s, way, t],
            device_id={"vec": sides[way]}, device_id_type=MESH)

    def rim(src, dst, s_sem, r_sem, i):
        return pltpu.make_async_remote_copy(
            src_ref=src.at[i], dst_ref=dst.at[1 - i],
            send_sem=s_sem.at[i], recv_sem=r_sem.at[1 - i],
            device_id={"rows": g + 1 - 2 * i}, device_id_type=MESH)

    own = [pltpu.make_async_copy(
        p_ref.at[s], ybuf.at[s, pl.ds(pl.multiple_of(me * shard, shard), shard), :],
        local_sem.at[s]) for s in range(sets)]

    barrier = pltpu.get_barrier_semaphore()
    for way in range(2):
        pl.semaphore_signal(barrier, inc=1, device_id={"vec": sides[way]}, device_id_type=MESH)

    @pl.when(has_up)
    def _():
        pl.semaphore_signal(barrier, inc=1, device_id={"rows": g + 1}, device_id_type=MESH)

    @pl.when(has_down)
    def _():
        pl.semaphore_signal(barrier, inc=1, device_id={"rows": g - 1}, device_id_type=MESH)

    for s in range(sets):
        own[s].start()
    edges = max(ng - 1, 1)
    peers = 2 + (edges - g + edges - 1) // edges + (g + edges - 1) // edges
    pl.semaphore_wait(barrier, peers)

    @pl.when(jnp.logical_not(has_up))
    def _():
        grecv[0] = jnp.zeros_like(grecv[0])
        wrecv[0] = jnp.zeros_like(wrecv[0])

    @pl.when(jnp.logical_not(has_down))
    def _():
        grecv[1] = jnp.zeros_like(grecv[1])
        wrecv[1] = jnp.zeros_like(wrecv[1])

    def forward(s, t):
        for way in range(2):
            if t > 0:
                arrived(s, t - 1, way).wait_recv()
            if t < steps:
                sent(s, t, way).start()
        if t == steps:
            own[s].wait()

    order = sorted(((2 * t + 3 * s, s, t) for s in range(sets) for t in range(steps + 1)))
    order = [(0, 0), (1, 0)] + [e[1:] for e in order if e[1:] not in ((0, 0), (1, 0))]

    def run(upto):
        while order:
            event = order.pop(0)
            forward(*event)
            if event == upto:
                return

    def both(src, dst, s_sem, r_sem, act):
        @pl.when(has_up)
        def _():
            act(rim(src, dst, s_sem, r_sem, 0))

        @pl.when(has_down)
        def _():
            act(rim(src, dst, s_sem, r_sem, 1))

    def recv_both(src, dst, s_sem, r_sem):
        @pl.when(has_up)
        def _():
            pltpu.make_async_remote_copy(
                src_ref=src.at[0], dst_ref=dst.at[0], send_sem=s_sem.at[0],
                recv_sem=r_sem.at[0], device_id={"rows": g + 1},
                device_id_type=MESH).wait_recv()

        @pl.when(has_down)
        def _():
            pltpu.make_async_remote_copy(
                src_ref=src.at[1], dst_ref=dst.at[1], send_sem=s_sem.at[1],
                recv_sem=r_sem.at[1], device_id={"rows": g - 1},
                device_id_type=MESH).wait_recv()

    run((0, steps))
    y0 = ybuf[0] + eye_of(2 * width, width)
    y0t = split(y0.T)
    y0 = split(y0)
    gram0 = mm(y0t, y0)
    z = z_ref[...]
    w0 = mm(y0t, split(z))
    run((2, 2) if steps > 2 else (1, steps - 1))
    inv0, = invert_all([gram0])
    if (1, steps) in order:
        run((1, steps))
    ya = ybuf[1, width:, :] + eye_of(width, width)
    yb = ybuf[1, :width, :]
    yat, ybt, ya, yb = split(ya.T), split(yb.T), split(ya), split(yb)
    gram_a = mm(yat, ya)
    gram_b = mm(ybt, yb)
    gsend[0] = gram_a
    gsend[1] = gram_b
    both(gsend, grecv, gs_sem, gr_sem, lambda copy: copy.start())
    run((2, steps - 1))
    z = z - mm(y0, split(mm(split(inv0), split(w0))))
    za, zb = z[width:], z[:width]
    wa = mm(yat, split(za))
    wb = mm(ybt, split(zb))
    wsend[0] = wa
    wsend[1] = wb
    both(wsend, wrecv, ws_sem, wr_sem, lambda copy: copy.start())
    run((2, steps))
    y2 = ybuf[2] + eye_of(2 * width, width)
    y2t = split(y2.T)
    y2 = split(y2)
    gram2 = mm(y2t, y2)
    recv_both(gsend, grecv, gs_sem, gr_sem)
    inv_a, inv_b, inv2 = invert_all([gram_a + grecv[0], gram_b + grecv[1], gram2])
    recv_both(wsend, wrecv, ws_sem, wr_sem)
    xa = split(mm(split(inv_a), split(wa + wrecv[0])))
    xb = split(mm(split(inv_b), split(wb + wrecv[1])))
    za = jnp.where(has_up, za - mm(ya, xa), za)
    zb = jnp.where(has_down, zb - mm(yb, xb), zb)
    z = jnp.concatenate([zb, za], axis=0)
    x2 = mm(split(inv2), split(mm(y2t, split(z))))
    out_ref[...] = z - mm(y2, split(x2))

    for s in range(sets):
        for way in range(2):
            for t in range(steps):
                sent(s, t, way).wait_send()
    both(gsend, grecv, gs_sem, gr_sem, lambda copy: copy.wait_send())
    both(wsend, wrecv, ws_sem, wr_sem, lambda copy: copy.wait_send())


def local(n, ng, eigen_rows, panels):
    sets, shard, width = panels.shape
    rows, columns = eigen_rows.shape
    dma = pltpu.SemaphoreType.DMA
    return pl.pallas_call(
        functools.partial(kernel, n, ng),
        out_shape=jax.ShapeDtypeStruct(eigen_rows.shape, F32),
        in_specs=[pl.BlockSpec(memory_space=pltpu.VMEM), pl.BlockSpec(memory_space=pl.ANY)],
        out_specs=pl.BlockSpec(memory_space=pltpu.VMEM),
        scratch_shapes=[
            pltpu.VMEM((sets, n * shard, width), F32),
            pltpu.VMEM((2, width, width), F32),
            pltpu.VMEM((2, width, width), F32),
            pltpu.VMEM((2, width, columns), F32),
            pltpu.VMEM((2, width, columns), F32),
            dma((sets,)),
            dma((sets, 2, n // 2)),
            dma((sets, 2, n // 2)),
            dma((2,)), dma((2,)), dma((2,)), dma((2,)),
        ],
        compiler_params=pltpu.CompilerParams(
            collective_id=0, has_side_effects=True, vmem_limit_bytes=48 * 2**20
        ),
        name="sweeps",
    )(eigen_rows, panels)


def solution(mesh):
    in_specs = (P("rows", "vec"), P(None, ("rows", "vec"), None))
    return jax.shard_map(
        functools.partial(local, mesh.shape["vec"], mesh.shape["rows"]),
        mesh=mesh, in_specs=in_specs, out_specs=P("rows", "vec"), check_vma=False)
```

time: 305 us -> 40.3 us (0.13)
  the two profiles are of different devices: /device:TPU:1 before, /device:TPU:0 now
where the time goes in v1:
time: 40.3 us; the launch traced here: 40.1 us
  Pallas kernels  37.5 us (93%)
  local copies, waits for them, and re-layouts  2.58 us (6%)
    pallas_call x1, Pallas kernels, local(): pl.pallas_call(functools.partial(kernel, n, ng), out_shape=jax.ShapeDtype...  37.5 us
    unnamed x5, local copies, waits for them, and re-layouts  2.58 us

profile of v1, /device:TPU:0, one launch (start us, length us, event | category | flops | bytes accessed | tf_op | source)
XLA Modules:
  0.0 40.1 jit_solution(12844323565008388757)
XLA Ops:
  0.0 0.0 copy-start
  0.0 0.9 %copy-done = f32[512,128]{1,0:T(8,128)S(1)} copy-done((f32[512,128]{1,0:T(8,128)S(1)}, f32[512,128]{1,0:T(8,128)}, u32[]{:S(2)}) %copy-start) | copy-done | bytes 262168
  1.0 0.0 copy-start.1
  1.0 0.9 %copy-done.1 = f32[3,64,256]{2,1,0:T(8,128)S(1)} copy-done((f32[3,64,256]{2,1,0:T(8,128)S(1)}, f32[3,64,256]{2,1,0:T(8,128)}, u32[]{:S(2)}) %copy-start.1) | copy-done | bytes 196632
  1.9 37.5 %sweeps.1 = f32[512,128]{1,0:T(8,128)S(1)} custom-call(f32[512,128]{1,0:T(8,128)S(1)} %copy-done, f32[3,64,256]{2,1,0:T(8,128)S(1)} %copy-done.1), custom_call_target="tpu_custom_call" | custom-call | tf_op jit(solution)/shard_map/sweeps/pallas_call | solution.py:269
  39.4 0.7 %copy.4 = f32[512,128]{1,0:T(8,128)} copy(f32[512,128]{1,0:T(8,128)S(1)} %sweeps.1) | data formatting | bytes 524288
Async XLA Ops:
  0.0 0.9 %copy-start = (f32[512,128]{1,0:T(8,128)S(1)}, f32[512,128]{1,0:T(8,128)}, u32[]{:S(2)}) copy-start(f32[512,128]{1,0:T(8,128)} %z_ref.1) | copy-start | bytes 786436
  1.0 0.9 %copy-start.1 = (f32[3,64,256]{2,1,0:T(8,128)S(1)}, f32[3,64,256]{2,1,0:T(8,128)}, u32[]{:S(2)}) copy-start(f32[3,64,256]{2,1,0:T(8,128)} %p_ref.1) | copy-start | bytes 589828

commit v2 on v1

--- a/solution.py
+++ b/solution.py
@@ -38,9 +38,14 @@
     return jnp.where(r == c, 1.0, 0.0).astype(F32)
 
 
+def upper(gram):
+    half = gram.shape[0] // 2
+    return jnp.concatenate(
+        [gram[:half, :half], gram[:half, half:], gram[half:, half:]], axis=0)
+
+
 def invert_all(grams):
-    width = grams[0].shape[0]
-    half = width // 2
+    half = grams[0].shape[1]
     r = lax.broadcasted_iota(jnp.int32, (half, half), 0)
     c = lax.broadcasted_iota(jnp.int32, (half, half), 1)
     eye = jnp.where(r == c, 1.0, 0.0).astype(F32)
@@ -49,12 +54,12 @@
         d_rows = []
         d_cols = []
         for i in range(2):
-            tile = g[i * half : (i + 1) * half, i * half : (i + 1) * half]
+            tile = g[2 * i * half : (2 * i + 1) * half]
             diag = jnp.where(r == c, 0.5 * tile, 0.0)
             d_rows.append(1.0 / jnp.sum(diag, axis=0, keepdims=True))
             d_cols.append(1.0 / jnp.sum(diag, axis=1, keepdims=True))
             parts.append(jnp.where(c > r, tile * d_rows[i], 0.0))
-        corners.append(g[:half, half:] * d_rows[1])
+        corners.append(g[half : 2 * half] * d_rows[1])
         scales.append(d_cols)
     small = [jnp.where(r // BASE == c // BASE, m, 0.0) for m in parts]
     pairs = [split(m) for m in small]
@@ -88,7 +93,7 @@
     return out
 
 
-def kernel(n, ng, z_ref, p_ref, out_ref, ybuf, gsend, grecv, wsend, wrecv,
+def kernel(n, ng, z_ref, p_ref, out_ref, zbuf, z_sem, ybuf, gsend, grecv, wsend, wrecv,
            local_sem, send_sem, recv_sem, gs_sem, gr_sem, ws_sem, wr_sem):
     sets, shard, width = p_ref.shape
     steps = n // 2
@@ -154,6 +159,8 @@
 
     for s in range(sets):
         own[s].start()
+    z_copy = pltpu.make_async_copy(z_ref, zbuf, z_sem)
+    z_copy.start()
     edges = max(ng - 1, 1)
     peers = 2 + (edges - g + edges - 1) // edges + (g + edges - 1) // edges
     pl.semaphore_wait(barrier, peers)
@@ -177,8 +184,10 @@
         if t == steps:
             own[s].wait()
 
-    order = sorted(((2 * t + 3 * s, s, t) for s in range(sets) for t in range(steps + 1)))
-    order = [(0, 0), (1, 0)] + [e[1:] for e in order if e[1:] not in ((0, 0), (1, 0))]
+    ranks = {1: 0, 0: 1, 2: 2}
+    order = sorted((2 * t + ranks[s] if t else 0, ranks[s], s, t)
+                   for s in range(sets) for t in range(steps + 1))
+    order = [e[2:] for e in order]
 
     def run(upto):
         while order:
@@ -211,26 +220,24 @@
                 recv_sem=r_sem.at[1], device_id={"rows": g - 1},
                 device_id_type=MESH).wait_recv()
 
+    run((1, steps))
+    run((2, steps - 1))
+    ya = ybuf[1, width:, :] + eye_of(width, width)
+    yb = ybuf[1, :width, :]
+    yat, ybt, ya, yb = split(ya.T), split(yb.T), split(ya), split(yb)
+    gram_a = upper(mm(yat, ya))
+    gram_b = upper(mm(ybt, yb))
+    gsend[0] = gram_a
+    gsend[1] = gram_b
+    both(gsend, grecv, gs_sem, gr_sem, lambda copy: copy.start())
+    z_copy.wait()
+    z = zbuf[...]
     run((0, steps))
     y0 = ybuf[0] + eye_of(2 * width, width)
     y0t = split(y0.T)
     y0 = split(y0)
-    gram0 = mm(y0t, y0)
-    z = z_ref[...]
     w0 = mm(y0t, split(z))
-    run((2, 2) if steps > 2 else (1, steps - 1))
-    inv0, = invert_all([gram0])
-    if (1, steps) in order:
-        run((1, steps))
-    ya = ybuf[1, width:, :] + eye_of(width, width)
-    yb = ybuf[1, :width, :]
-    yat, ybt, ya, yb = split(ya.T), split(yb.T), split(ya), split(yb)
-    gram_a = mm(yat, ya)
-    gram_b = mm(ybt, yb)
-    gsend[0] = gram_a
-    gsend[1] = gram_b
-    both(gsend, grecv, gs_sem, gr_sem, lambda copy: copy.start())
-    run((2, steps - 1))
+    inv0, = invert_all([upper(mm(y0t, y0))])
     z = z - mm(y0, split(mm(split(inv0), split(w0))))
     za, zb = z[width:], z[:width]
     wa = mm(yat, split(za))
@@ -242,7 +249,7 @@
     y2 = ybuf[2] + eye_of(2 * width, width)
     y2t = split(y2.T)
     y2 = split(y2)
-    gram2 = mm(y2t, y2)
+    gram2 = upper(mm(y2t, y2))
     recv_both(gsend, grecv, gs_sem, gr_sem)
     inv_a, inv_b, inv2 = invert_all([gram_a + grecv[0], gram_b + grecv[1], gram2])
     recv_both(wsend, wrecv, ws_sem, wr_sem)
@@ -269,12 +276,14 @@
     return pl.pallas_call(
         functools.partial(kernel, n, ng),
         out_shape=jax.ShapeDtypeStruct(eigen_rows.shape, F32),
-        in_specs=[pl.BlockSpec(memory_space=pltpu.VMEM), pl.BlockSpec(memory_space=pl.ANY)],
+        in_specs=[pl.BlockSpec(memory_space=pl.ANY)] * 2,
         out_specs=pl.BlockSpec(memory_space=pltpu.VMEM),
         scratch_shapes=[
+            pltpu.VMEM((rows, columns), F32),
+            dma(()),
             pltpu.VMEM((sets, n * shard, width), F32),
-            pltpu.VMEM((2, width, width), F32),
-            pltpu.VMEM((2, width, width), F32),
+            pltpu.VMEM((2, width // 2 * 3, width // 2), F32),
+            pltpu.VMEM((2, width // 2 * 3, width // 2), F32),
             pltpu.VMEM((2, width, columns), F32),
             pltpu.VMEM((2, width, columns), F32),
             dma((sets,)),

time: 40.3 us -> 34.5 us (0.86)
  the two profiles are of different devices: /device:TPU:0 before, /device:TPU:1 now
where the time goes in v2:
time: 34.5 us; the launch traced here: 34.3 us
  Pallas kernels  31.8 us (92%)
  local copies, waits for them, and re-layouts  2.58 us (7%)
    pallas_call x1, Pallas kernels, local(): pl.pallas_call(functools.partial(kernel, n, ng), out_shape=jax.ShapeDtype...  31.8 us
    unnamed x5, local copies, waits for them, and re-layouts  2.58 us

profile of v2, /device:TPU:1, one launch (start us, length us, event | category | flops | bytes accessed | tf_op | source)
XLA Modules:
  0.0 34.3 jit_solution(7474093111503098932)
XLA Ops:
  0.0 0.0 copy-start
  0.0 0.9 %copy-done = f32[512,128]{1,0:T(8,128)S(1)} copy-done((f32[512,128]{1,0:T(8,128)S(1)}, f32[512,128]{1,0:T(8,128)}, u32[]{:S(2)}) %copy-start) | copy-done | bytes 262168
  1.0 0.0 copy-start.1
  1.0 0.9 %copy-done.1 = f32[3,64,256]{2,1,0:T(8,128)S(1)} copy-done((f32[3,64,256]{2,1,0:T(8,128)S(1)}, f32[3,64,256]{2,1,0:T(8,128)}, u32[]{:S(2)}) %copy-start.1) | copy-done | bytes 196632
  1.9 31.8 %sweeps.1 = f32[512,128]{1,0:T(8,128)S(1)} custom-call(f32[512,128]{1,0:T(8,128)S(1)} %copy-done, f32[3,64,256]{2,1,0:T(8,128)S(1)} %copy-done.1), custom_call_target="tpu_custom_call" | custom-call | tf_op jit(solution)/shard_map/sweeps/pallas_call | solution.py:276
  33.6 0.7 %copy.4 = f32[512,128]{1,0:T(8,128)} copy(f32[512,128]{1,0:T(8,128)S(1)} %sweeps.1) | data formatting | bytes 524288
Async XLA Ops:
  0.0 0.9 %copy-start = (f32[512,128]{1,0:T(8,128)S(1)}, f32[512,128]{1,0:T(8,128)}, u32[]{:S(2)}) copy-start(f32[512,128]{1,0:T(8,128)} %z_ref.1) | copy-start | bytes 786436
  1.0 0.9 %copy-start.1 = (f32[3,64,256]{2,1,0:T(8,128)S(1)}, f32[3,64,256]{2,1,0:T(8,128)}, u32[]{:S(2)}) copy-start(f32[3,64,256]{2,1,0:T(8,128)} %p_ref.1) | copy-start | bytes 589828
